TPU v7x, 512 devices: a whole 4x8x8 slice. The times are simulated.
512 devices in a mesh: delay: 16 (over y, core), row: 32 (over z, x).
Axes of the slice: x: 4, y: 8, z: 8, core: 2. Of those that a mesh axis runs over, the one named last changes fastest.
Arguments:
- incident: bfloat16 [64, 4096], P(None, 'row'), may hold values from -12 to 12
- onset: int32 [64], replicated, may hold values from 0 to 2
- beta: float32 [4096], P('delay'), may hold values from 0.05 to 0.5
- inverse_block: bfloat16 [4096, 4096], P('row', 'delay'), may hold values from -0.0625 to 0.0625
- delay_blocks: bfloat16 [16, 4096, 4096], P('delay', None, 'row'), may hold values from -0.09375 to 0.09375
- history_sum: float32 [16, 64, 4096], P('delay', None, 'row'), may hold values from -12 to 12
Outputs:
- currents: bfloat16 [3, 64, 4096], P(None, None, 'delay')
- carried: float32 [16, 64, 4096], P('delay', None, 'row')
All inputs are finite; a program needn't handle non-finite values.
Results may differ from a plain program's by a relative error of at most 0.0056.
Values may be sent and summed in bfloat16 or wider, within the bound.
A program may use at most 64 MiB of HBM per device.

v0:
```python
import jax
import jax.numpy as jnp
from jax import lax
from jax.sharding import PartitionSpec as P

STEPS = 3


def broadcast(value, axis, root):
    return lax.dynamic_index_in_dim(lax.all_gather(value, axis), root, 0, keepdims=False)


def in_blocks(value, dim, devices):
    dims = value.shape
    blocks = value.reshape(*dims[:dim], devices, dims[dim] // devices, *dims[dim + 1 :])
    return jnp.moveaxis(blocks, dim, 0)


def sent_and_summed(value, axis, dim):
    devices = lax.axis_size(axis)
    blocks = lax.all_to_all(in_blocks(value, dim, devices), axis, 0, 0, tiled=True)
    return jnp.sum(blocks, axis=0)


def copy_for_each(value, axis):
    copies = jnp.broadcast_to(value, (lax.axis_size(axis), *value.shape))
    return lax.all_to_all(copies, axis, split_axis=0, concat_axis=0, tiled=True)


def joined_along(blocks, dim):
    blocks = jnp.moveaxis(blocks, 0, dim)
    dims = blocks.shape
    return blocks.reshape(*dims[:dim], dims[dim] * dims[dim + 1], *dims[dim + 2 :])


def gathered_copies(value, axis, dim):
    blocks = copy_for_each(value, axis)
    return joined_along(blocks, dim)


def passed_along(value, axis, by):
    devices = lax.axis_size(axis)
    pairs = [(i, i + by) for i in range(devices) if 0 <= i + by < devices]
    return lax.ppermute(value, axis, pairs)


def per_device(incident, onset, beta, inverse_block, delay_blocks, history_sum):
    future = history_sum[0]
    matrix = delay_blocks[0]
    incident_wide = incident.astype(jnp.float32)
    outputs = []
    for step_index in range(STEPS):
        offset_time = (step_index - onset).astype(jnp.float32)
        envelope = jnp.where(offset_time >= 0.0, jnp.exp(-((offset_time - 1.0) ** 2) / 4.0), 0.0)
        residual = (incident_wide * envelope[:, None] - future).astype(jnp.bfloat16)
        residual = broadcast(residual, "delay", 0)
        partial_sum = jnp.dot(residual, inverse_block, preferred_element_type=jnp.float32)
        solved = sent_and_summed(partial_sum, "row", 0)
        current = (solved / (1.0 + beta[None, :] * solved * solved)).astype(jnp.bfloat16)
        own_block = gathered_copies(current, "row", 0)
        gathered = lax.all_gather(own_block, "delay", axis=1, tiled=True)
        outputs.append(own_block)
        passed = passed_along(future, "delay", -1)
        future = passed + jnp.dot(gathered, matrix, preferred_element_type=jnp.float32)
    return (jnp.stack(outputs), future[None])


def solution(mesh):
    placed = (
        P(None, "row"),
        P(),
        P("delay"),
        P("row", "delay"),
        P("delay", None, "row"),
        P("delay", None, "row"),
    )
    return jax.shard_map(
        per_device,
        mesh=mesh,
        in_specs=placed,
        out_specs=(P(None, None, "delay"), P("delay", None, "row")),
        check_vma=False,
    )
```

profile of v0, /device:TPU:1, one launch (start us, length us, event | category | flops | bytes accessed | tf_op | source)
XLA Modules:
  0.0 199.1 jit_solution(9493592428893358727)
XLA Ops:
  0.6 0.8 compare_select_fusion.1
  1.4 0.9 fusion.12
  2.3 21.7 %all-gather = bf16[1024,128]{1,0:T(8,128)(2,1)S(1)} all-gather(bf16[64,128]{1,0:T(8,128)(2,1)S(1)} %fusion.12), channel_id=2, replica_groups=mesh['delay'=16,'row'=32] {'delay'}, dimensions={0}, use_global_device_ids=true | all-gather | bytes 278528 | tf_op jit(solution)/shard_map/all_gather | solution.py:10
  24.2 19.6 %all_to_all.30 = f32[32,2,256]{2,1,0:T(2,128)S(1)} all-to-all(f32[32,2,256]{2,1,0:T(2,128)S(1)} %copy.14), channel_id=1, replica_groups=mesh['delay'=16,'row'=32] {'row'}, dimensions={0} | all-to-all | bytes 131072 | tf_op jit(solution)/shard_map/all_to_all | solution.py:21
  44.5 0.6 broadcast_in_dim.22
  45.1 4.0 %all-to-all-start.1 = ((bf16[32,2,256]{2,1,0:T(2,128)(2,1)}), bf16[32,2,256]{2,1,0:T(2,128)(2,1)S(1)}, u32[]{:S(2)}, u32[]{:S(2)}) async-start(bf16[32,2,256]{2,1,0:T(2,128)(2,1)} %broadcast_in_dim.22), calls=%async_computation.1 | async-start | bytes 65536 | tf_op jit(solution)/shard_map/all_to_all | solution.py:27
  49.1 3.5 %collective-permute-start = (f32[64,128]{1,0:T(8,128)S(1)}, f32[64,128]{1,0:T(8,128)S(1)}, u32[]{:S(2)}, u32[]{:S(2)}) collective-permute-start(f32[64,128]{1,0:T(8,128)S(1)} %bitcast.29), channel_id=1, source_target_pairs={{32,0},{64,32},{96,64},{128,96},{160,128},{192,160},{224,192},{256... | collective-permute-start | bytes 98312 | tf_op jit(solution)/shard_map/ppermute | solution.py:44
  52.6 5.1 %all-to-all-done.1 = bf16[32,2,256]{2,1,0:T(2,128)(2,1)S(1)} async-done(((bf16[32,2,256]{2,1,0:T(2,128)(2,1)}), bf16[32,2,256]{2,1,0:T(2,128)(2,1)S(1)}, u32[]{:S(2)}, u32[]{:S(2)}) %all-to-all-start.1) | async-done | bytes 32800 | tf_op jit(solution)/shard_map/all_to_all | solution.py:27
  57.8 18.9 %all_gather.29 = bf16[64,4096]{1,0:T(8,128)(2,1)S(1)} all-gather(bf16[64,256]{1,0:T(8,128)(2,1)S(1)} %reshape.26), channel_id=1, replica_groups=mesh['delay'=16,'row'=32] {'delay'}, dimensions={1}, use_global_device_ids=true | all-gather | bytes 557056 | tf_op jit(solution)/shard_map/all_gather | solution.py:61
  77.0 16.0 %all-gather.1 = bf16[1024,128]{1,0:T(8,128)(2,1)S(1)} all-gather(bf16[64,128]{1,0:T(8,128)(2,1)S(1)} %get-tuple-element.7), channel_id=3, replica_groups=mesh['delay'=16,'row'=32] {'delay'}, dimensions={0}, use_global_device_ids=true | all-gather | bytes 278528 | tf_op jit(solution)/shard_map/all_gather | solution.py:10
  93.3 11.8 %all_to_all.31 = f32[32,2,256]{2,1,0:T(2,128)S(1)} all-to-all(f32[32,2,256]{2,1,0:T(2,128)S(1)} %copy.16), channel_id=1, replica_groups=mesh['delay'=16,'row'=32] {'row'}, dimensions={0} | all-to-all | bytes 131072 | tf_op jit(solution)/shard_map/all_to_all | solution.py:21
  105.2 0.6 broadcast_in_dim.23
  105.8 3.9 %all-to-all-start.3 = ((bf16[32,2,256]{2,1,0:T(2,128)(2,1)}), bf16[32,2,256]{2,1,0:T(2,128)(2,1)S(1)}, u32[]{:S(2)}, u32[]{:S(2)}) async-start(bf16[32,2,256]{2,1,0:T(2,128)(2,1)} %broadcast_in_dim.23), calls=%async_computation.3 | async-start | bytes 65536 | tf_op jit(solution)/shard_map/all_to_all | solution.py:27
  109.7 3.3 %collective-permute-start.1 = (f32[64,128]{1,0:T(8,128)S(1)}, f32[64,128]{1,0:T(8,128)S(1)}, u32[]{:S(2)}, u32[]{:S(2)}) collective-permute-start(f32[64,128]{1,0:T(8,128)S(1)} %get-tuple-element.8), channel_id=1, source_target_pairs={{32,0},{64,32},{96,64},{128,96},{160,128},{192,160},{224,192},{256... | collective-permute-start | bytes 98312 | tf_op jit(solution)/shard_map/ppermute | solution.py:44
  113.0 5.3 %all-to-all-done.3 = bf16[32,2,256]{2,1,0:T(2,128)(2,1)S(1)} async-done(((bf16[32,2,256]{2,1,0:T(2,128)(2,1)}), bf16[32,2,256]{2,1,0:T(2,128)(2,1)S(1)}, u32[]{:S(2)}, u32[]{:S(2)}) %all-to-all-start.3) | async-done | bytes 32800 | tf_op jit(solution)/shard_map/all_to_all | solution.py:27
  118.3 18.7 %all_gather.32 = bf16[64,4096]{1,0:T(8,128)(2,1)S(1)} all-gather(bf16[64,256]{1,0:T(8,128)(2,1)S(1)} %reshape.27), channel_id=1, replica_groups=mesh['delay'=16,'row'=32] {'delay'}, dimensions={1}, use_global_device_ids=true | all-gather | bytes 557056 | tf_op jit(solution)/shard_map/all_gather | solution.py:61
  137.5 16.0 %all-gather.2 = bf16[1024,128]{1,0:T(8,128)(2,1)S(1)} all-gather(bf16[64,128]{1,0:T(8,128)(2,1)S(1)} %get-tuple-element.2), channel_id=4, replica_groups=mesh['delay'=16,'row'=32] {'delay'}, dimensions={0}, use_global_device_ids=true | all-gather | bytes 278528 | tf_op jit(solution)/shard_map/all_gather | solution.py:10
  153.7 11.8 %all_to_all.32 = f32[32,2,256]{2,1,0:T(2,128)S(1)} all-to-all(f32[32,2,256]{2,1,0:T(2,128)S(1)} %copy.18), channel_id=1, replica_groups=mesh['delay'=16,'row'=32] {'row'}, dimensions={0} | all-to-all | bytes 131072 | tf_op jit(solution)/shard_map/all_to_all | solution.py:21
  165.6 0.6 broadcast_in_dim.24
  166.2 3.9 %all-to-all-start.5 = ((bf16[32,2,256]{2,1,0:T(2,128)(2,1)}), bf16[32,2,256]{2,1,0:T(2,128)(2,1)S(1)}, u32[]{:S(2)}, u32[]{:S(2)}) async-start(bf16[32,2,256]{2,1,0:T(2,128)(2,1)} %broadcast_in_dim.24), calls=%async_computation.5 | async-start | bytes 65536 | tf_op jit(solution)/shard_map/all_to_all | solution.py:27
  170.1 3.3 %collective-permute-start.2 = (f32[64,128]{1,0:T(8,128)S(1)}, f32[64,128]{1,0:T(8,128)S(1)}, u32[]{:S(2)}, u32[]{:S(2)}) collective-permute-start(f32[64,128]{1,0:T(8,128)S(1)} %get-tuple-element.3), channel_id=1, source_target_pairs={{32,0},{64,32},{96,64},{128,96},{160,128},{192,160},{224,192},{256... | collective-permute-start | bytes 98312 | tf_op jit(solution)/shard_map/ppermute | solution.py:44
  173.4 5.3 %all-to-all-done.5 = bf16[32,2,256]{2,1,0:T(2,128)(2,1)S(1)} async-done(((bf16[32,2,256]{2,1,0:T(2,128)(2,1)}), bf16[32,2,256]{2,1,0:T(2,128)(2,1)S(1)}, u32[]{:S(2)}, u32[]{:S(2)}) %all-to-all-start.5) | async-done | bytes 32800 | tf_op jit(solution)/shard_map/all_to_all | solution.py:27
  178.7 18.7 %all_gather.35 = bf16[64,4096]{1,0:T(8,128)(2,1)S(1)} all-gather(bf16[64,256]{1,0:T(8,128)(2,1)S(1)} %reshape.28), channel_id=1, replica_groups=mesh['delay'=16,'row'=32] {'delay'}, dimensions={1}, use_global_device_ids=true | all-gather | bytes 557056 | tf_op jit(solution)/shard_map/all_gather | solution.py:61
  197.8 0.7 pad_maximum_fusion
  (39 shorter events, 3.2 us)
Async XLA Ops:
  0.6 76.0 %copy-start = (bf16[1,4096,128]{2,1,0:T(8,128)(2,1)S(1)}, bf16[1,4096,128]{2,1,0:T(8,128)(2,1)}, u32[]{:S(2)}) copy-start(bf16[1,4096,128]{2,1,0:T(8,128)(2,1)} %param.10) | copy-start | bytes 3145732
  2.3 21.7 %copy-start.1 = (bf16[128,256]{1,0:T(8,128)(2,1)S(1)}, bf16[128,256]{1,0:T(8,128)(2,1)}, u32[]{:S(2)}) copy-start(bf16[128,256]{1,0:T(8,128)(2,1)} %param.9) | copy-start | bytes 196612
  43.8 0.7 copy-start.4
  45.1 4.0 %copy-start.3 = (f32[1,64,128]{2,1,0:T(8,128)S(1)}, f32[1,64,128]{2,1,0:T(8,128)}, u32[]{:S(2)}) copy-start(f32[1,64,128]{2,1,0:T(8,128)} %param.11) | copy-start | bytes 98308
  45.1 12.6 %all-to-all-start.1 = ((bf16[32,2,256]{2,1,0:T(2,128)(2,1)}), bf16[32,2,256]{2,1,0:T(2,128)(2,1)S(1)}, u32[]{:S(2)}, u32[]{:S(2)}) async-start(bf16[32,2,256]{2,1,0:T(2,128)(2,1)} %broadcast_in_dim.22), calls=%async_computation.1 | async-start | bytes 65536 | tf_op jit(solution)/shard_map/all_to_all | solution.py:27
  49.1 27.6 %collective-permute-start = (f32[64,128]{1,0:T(8,128)S(1)}, f32[64,128]{1,0:T(8,128)S(1)}, u32[]{:S(2)}, u32[]{:S(2)}) collective-permute-start(f32[64,128]{1,0:T(8,128)S(1)} %bitcast.29), channel_id=1, source_target_pairs={{32,0},{64,32},{96,64},{128,96},{160,128},{192,160},{224,192},{256... | collective-permute-start | bytes 98312 | tf_op jit(solution)/shard_map/ppermute | solution.py:44
  57.7 18.9 %copy-start.2 = (bf16[64,128]{1,0:T(8,128)(2,1)S(1)}, bf16[64,128]{1,0:T(8,128)(2,1)}, u32[]{:S(2)}) copy-start(bf16[64,128]{1,0:T(8,128)(2,1)} %param.6) | copy-start | bytes 49156
  105.8 12.5 %all-to-all-start.3 = ((bf16[32,2,256]{2,1,0:T(2,128)(2,1)}), bf16[32,2,256]{2,1,0:T(2,128)(2,1)S(1)}, u32[]{:S(2)}, u32[]{:S(2)}) async-start(bf16[32,2,256]{2,1,0:T(2,128)(2,1)} %broadcast_in_dim.23), calls=%async_computation.3 | async-start | bytes 65536 | tf_op jit(solution)/shard_map/all_to_all | solution.py:27
  109.7 27.7 %collective-permute-start.1 = (f32[64,128]{1,0:T(8,128)S(1)}, f32[64,128]{1,0:T(8,128)S(1)}, u32[]{:S(2)}, u32[]{:S(2)}) collective-permute-start(f32[64,128]{1,0:T(8,128)S(1)} %get-tuple-element.8), channel_id=1, source_target_pairs={{32,0},{64,32},{96,64},{128,96},{160,128},{192,160},{224,192},{256... | collective-permute-start | bytes 98312 | tf_op jit(solution)/shard_map/ppermute | solution.py:44
  166.2 12.5 %all-to-all-start.5 = ((bf16[32,2,256]{2,1,0:T(2,128)(2,1)}), bf16[32,2,256]{2,1,0:T(2,128)(2,1)S(1)}, u32[]{:S(2)}, u32[]{:S(2)}) async-start(bf16[32,2,256]{2,1,0:T(2,128)(2,1)} %broadcast_in_dim.24), calls=%async_computation.5 | async-start | bytes 65536 | tf_op jit(solution)/shard_map/all_to_all | solution.py:27
  170.1 28.4 %collective-permute-start.2 = (f32[64,128]{1,0:T(8,128)S(1)}, f32[64,128]{1,0:T(8,128)S(1)}, u32[]{:S(2)}, u32[]{:S(2)}) collective-permute-start(f32[64,128]{1,0:T(8,128)S(1)} %get-tuple-element.3), channel_id=1, source_target_pairs={{32,0},{64,32},{96,64},{128,96},{160,128},{192,160},{224,192},{256... | collective-permute-start | bytes 98312 | tf_op jit(solution)/shard_map/ppermute | solution.py:44
where the time goes:
time: 200 us; the launch traced here: 199 us
  blocking collectives  153 us (76%)
  starting transfers between devices  21.8 us (11%)
  waiting for transfers between devices  15.7 us (8%)
  other arithmetic  3.13 us (2%)
  local copies, waits for them, and re-layouts  2.87 us (1%)
    all_gather x3, blocking collectives, per_device(): gathered = lax.all_gather(own_block, 'delay', axis=1, tiled=True)  56.4 us
    all_gather x3, blocking collectives, broadcast(): lax.all_gather(value, axis)  53.8 us
    all_to_all x3, blocking collectives, sent_and_summed(): lax.all_to_all(in_blocks(value, dim, devices), axis, 0, 0, tiled=True)  43.3 us
    all_to_all x3, waiting for transfers between devices, copy_for_each(): return lax.all_to_all(copies, axis, split_axis=0, concat_axis=0, tiled=True)  15.7 us
    all_to_all x3, starting transfers between devices, copy_for_each(): return lax.all_to_all(copies, axis, split_axis=0, concat_axis=0, tiled=True)  11.7 us
    ppermute x3, starting transfers between devices, passed_along(): return lax.ppermute(value, axis, pairs)  10.1 us
  transfers between devices with their start and end apart: 6, of which 3 were waited for; matrix products, arithmetic and copies ran while one was open for 1% of the time, Pallas kernels for 0%

commit v1 on v0

--- a/solution.py
+++ b/solution.py
@@ -4,6 +4,11 @@
 from jax.sharding import PartitionSpec as P
 
 STEPS = 3
+
+
+def gather_over(shard, axis, along):
+    sent = jnp.stack([shard] * lax.axis_size(axis))
+    return jnp.concatenate(lax.all_to_all(sent, axis, 0, 0), axis=along)
 
 
 def broadcast(value, axis, root):
@@ -58,7 +63,7 @@
         solved = sent_and_summed(partial_sum, "row", 0)
         current = (solved / (1.0 + beta[None, :] * solved * solved)).astype(jnp.bfloat16)
         own_block = gathered_copies(current, "row", 0)
-        gathered = lax.all_gather(own_block, "delay", axis=1, tiled=True)
+        gathered = gather_over(own_block, "delay", 1)
         outputs.append(own_block)
         passed = passed_along(future, "delay", -1)
         future = passed + jnp.dot(gathered, matrix, preferred_element_type=jnp.float32)

time: 200 us -> 215 us (1.075)
  waiting for transfers between devices: 15.7 us -> 45.2 us
  blocking collectives: 153 us -> 131 us
  starting transfers between devices: 21.8 us -> 28.1 us
    all_gather x3 -> x0, blocking collectives: 56.4 us -> none  [per_device(): gathered = lax.all_gather(own_block, 'delay', axis=1, tiled=True)]
    all_to_all x0 -> x3, blocking collectives: none -> 35.3 us  [copy_for_each(): return lax.all_to_all(copies, axis, split_axis=0, concat_axis=0, tiled=True)]
    all_to_all x3, waiting for transfers between devices: 15.7 us -> 45.2 us  [gather_over(): return jnp.concatenate(lax.all_to_all(sent, axis, 0, 0), axis=along)]
    all_to_all x3, starting transfers between devices: 11.7 us -> 22.1 us  [gather_over(): return jnp.concatenate(lax.all_to_all(sent, axis, 0, 0), axis=along)]
    ppermute x3, starting transfers between devices: 10.1 us -> 6.04 us  [passed_along(): return lax.ppermute(value, axis, pairs)]
    another operation x0 -> x3, local copies, waits for them, and re-layouts: none -> 2.57 us  [gather_over(): sent = jnp.stack([shard] * lax.axis_size(axis))]
where the time goes in v1:
time: 215 us; the launch traced here: 214 us
  blocking collectives  131 us (61%)
  waiting for transfers between devices  45.2 us (21%)
  starting transfers between devices  28.1 us (13%)
  local copies, waits for them, and re-layouts  4.34 us (2%)
  other arithmetic  3.13 us (1%)
    all_gather x3, blocking collectives, broadcast(): lax.all_gather(value, axis)  52.1 us
    all_to_all x3, waiting for transfers between devices, gather_over(): return jnp.concatenate(lax.all_to_all(sent, axis, 0, 0), axis=along)  45.2 us
    all_to_all x3, blocking collectives, sent_and_summed(): lax.all_to_all(in_blocks(value, dim, devices), axis, 0, 0, tiled=True)  43.3 us
    all_to_all x3, blocking collectives, copy_for_each(): return lax.all_to_all(copies, axis, split_axis=0, concat_axis=0, tiled=True)  35.3 us
    all_to_all x3, starting transfers between devices, gather_over(): return jnp.concatenate(lax.all_to_all(sent, axis, 0, 0), axis=along)  22.1 us
    ppermute x3, starting transfers between devices, passed_along(): return lax.ppermute(value, axis, pairs)  6.04 us
  transfers between devices with their start and end apart: 6, of which 3 were waited for; matrix products, arithmetic and copies ran while one was open for 1% of the time, Pallas kernels for 0%

profile of v1, /device:TPU:1, one launch (start us, length us, event | category | flops | bytes accessed | tf_op | source)
XLA Modules:
  0.0 213.6 jit_solution(750109058452023752)
XLA Ops:
  0.6 0.8 compare_select_fusion.1
  1.4 0.9 fusion.12
  2.3 21.7 %all-gather = bf16[1024,128]{1,0:T(8,128)(2,1)S(1)} all-gather(bf16[64,128]{1,0:T(8,128)(2,1)S(1)} %fusion.12), channel_id=2, replica_groups=mesh['delay'=16,'row'=32] {'delay'}, dimensions={0}, use_global_device_ids=true | all-gather | bytes 278528 | tf_op jit(solution)/shard_map/all_gather | solution.py:15
  24.2 19.6 %all_to_all.45 = f32[32,2,256]{2,1,0:T(2,128)S(1)} all-to-all(f32[32,2,256]{2,1,0:T(2,128)S(1)} %copy.14), channel_id=1, replica_groups=mesh['delay'=16,'row'=32] {'row'}, dimensions={0} | all-to-all | bytes 131072 | tf_op jit(solution)/shard_map/all_to_all | solution.py:26
  44.5 11.8 %all_to_all.46 = bf16[32,2,256]{2,1,0:T(2,128)(2,1)S(1)} all-to-all(bf16[32,2,256]{2,1,0:T(2,128)(2,1)S(1)} %broadcast_in_dim.22), channel_id=1, replica_groups=mesh['delay'=16,'row'=32] {'row'}, dimensions={0} | all-to-all | bytes 65536 | tf_op jit(solution)/shard_map/all_to_all | solution.py:32
  56.3 0.9 stack.12
  57.2 7.2 %all-to-all-start.2 = ((bf16[16,64,256]{2,1,0:T(8,128)(2,1)}), bf16[16,64,256]{2,1,0:T(8,128)(2,1)S(1)}, u32[]{:S(2)}, u32[]{:S(2)}) async-start(bf16[16,64,256]{2,1,0:T(8,128)(2,1)} %stack.12), calls=%async_computation.2 | async-start | bytes 1048576 | tf_op jit(solution)/shard_map/all_to_all | solution.py:11
  64.3 2.0 collective-permute-start
  66.4 15.3 %all-to-all-done.2 = bf16[16,64,256]{2,1,0:T(8,128)(2,1)S(1)} async-done(((bf16[16,64,256]{2,1,0:T(8,128)(2,1)}), bf16[16,64,256]{2,1,0:T(8,128)(2,1)S(1)}, u32[]{:S(2)}, u32[]{:S(2)}) %all-to-all-start.2) | async-done | bytes 524320 | tf_op jit(solution)/shard_map/all_to_all | solution.py:11
  81.7 0.7 copy-done.2
  82.7 15.2 %all-gather.1 = bf16[1024,128]{1,0:T(8,128)(2,1)S(1)} all-gather(bf16[64,128]{1,0:T(8,128)(2,1)S(1)} %get-tuple-element.7), channel_id=3, replica_groups=mesh['delay'=16,'row'=32] {'delay'}, dimensions={0}, use_global_device_ids=true | all-gather | bytes 278528 | tf_op jit(solution)/shard_map/all_gather | solution.py:15
  98.1 11.9 %all_to_all.47 = f32[32,2,256]{2,1,0:T(2,128)S(1)} all-to-all(f32[32,2,256]{2,1,0:T(2,128)S(1)} %copy.17), channel_id=1, replica_groups=mesh['delay'=16,'row'=32] {'row'}, dimensions={0} | all-to-all | bytes 131072 | tf_op jit(solution)/shard_map/all_to_all | solution.py:26
  110.0 11.8 %all_to_all.48 = bf16[32,2,256]{2,1,0:T(2,128)(2,1)S(1)} all-to-all(bf16[32,2,256]{2,1,0:T(2,128)(2,1)S(1)} %broadcast_in_dim.23), channel_id=1, replica_groups=mesh['delay'=16,'row'=32] {'row'}, dimensions={0} | all-to-all | bytes 65536 | tf_op jit(solution)/shard_map/all_to_all | solution.py:32
  121.8 0.9 stack.13
  122.7 7.4 %all-to-all-start.5 = ((bf16[16,64,256]{2,1,0:T(8,128)(2,1)}), bf16[16,64,256]{2,1,0:T(8,128)(2,1)S(1)}, u32[]{:S(2)}, u32[]{:S(2)}) async-start(bf16[16,64,256]{2,1,0:T(8,128)(2,1)} %stack.13), calls=%async_computation.5 | async-start | bytes 1048576 | tf_op jit(solution)/shard_map/all_to_all | solution.py:11
  130.1 2.0 collective-permute-start.1
  132.1 15.3 %all-to-all-done.5 = bf16[16,64,256]{2,1,0:T(8,128)(2,1)S(1)} async-done(((bf16[16,64,256]{2,1,0:T(8,128)(2,1)}), bf16[16,64,256]{2,1,0:T(8,128)(2,1)S(1)}, u32[]{:S(2)}, u32[]{:S(2)}) %all-to-all-start.5) | async-done | bytes 524320 | tf_op jit(solution)/shard_map/all_to_all | solution.py:11
  147.9 15.2 %all-gather.2 = bf16[1024,128]{1,0:T(8,128)(2,1)S(1)} all-gather(bf16[64,128]{1,0:T(8,128)(2,1)S(1)} %get-tuple-element.2), channel_id=4, replica_groups=mesh['delay'=16,'row'=32] {'delay'}, dimensions={0}, use_global_device_ids=true | all-gather | bytes 278528 | tf_op jit(solution)/shard_map/all_gather | solution.py:15
  163.3 11.9 %all_to_all.49 = f32[32,2,256]{2,1,0:T(2,128)S(1)} all-to-all(f32[32,2,256]{2,1,0:T(2,128)S(1)} %copy.20), channel_id=1, replica_groups=mesh['delay'=16,'row'=32] {'row'}, dimensions={0} | all-to-all | bytes 131072 | tf_op jit(solution)/shard_map/all_to_all | solution.py:26
  175.2 11.8 %all_to_all.50 = bf16[32,2,256]{2,1,0:T(2,128)(2,1)S(1)} all-to-all(bf16[32,2,256]{2,1,0:T(2,128)(2,1)S(1)} %broadcast_in_dim.24), channel_id=1, replica_groups=mesh['delay'=16,'row'=32] {'row'}, dimensions={0} | all-to-all | bytes 65536 | tf_op jit(solution)/shard_map/all_to_all | solution.py:32
  187.0 0.9 stack.15
  187.8 7.4 %all-to-all-start.8 = ((bf16[16,64,256]{2,1,0:T(8,128)(2,1)}), bf16[16,64,256]{2,1,0:T(8,128)(2,1)S(1)}, u32[]{:S(2)}, u32[]{:S(2)}) async-start(bf16[16,64,256]{2,1,0:T(8,128)(2,1)} %stack.15), calls=%async_computation.8 | async-start | bytes 1048576 | tf_op jit(solution)/shard_map/all_to_all | solution.py:11
  195.3 2.0 collective-permute-start.2
  198.0 14.6 %all-to-all-done.8 = bf16[16,64,256]{2,1,0:T(8,128)(2,1)S(1)} async-done(((bf16[16,64,256]{2,1,0:T(8,128)(2,1)}), bf16[16,64,256]{2,1,0:T(8,128)(2,1)S(1)}, u32[]{:S(2)}, u32[]{:S(2)}) %all-to-all-start.8) | async-done | bytes 524320 | tf_op jit(solution)/shard_map/all_to_all | solution.py:11
  (45 shorter events, 4.0 us)
Async XLA Ops:
  0.6 81.1 %copy-start = (bf16[1,4096,128]{2,1,0:T(8,128)(2,1)S(1)}, bf16[1,4096,128]{2,1,0:T(8,128)(2,1)}, u32[]{:S(2)}) copy-start(bf16[1,4096,128]{2,1,0:T(8,128)(2,1)} %param.10) | copy-start | bytes 3145732
  2.3 21.7 %copy-start.1 = (bf16[128,256]{1,0:T(8,128)(2,1)S(1)}, bf16[128,256]{1,0:T(8,128)(2,1)}, u32[]{:S(2)}) copy-start(bf16[128,256]{1,0:T(8,128)(2,1)} %param.9) | copy-start | bytes 196612
  43.8 0.7 copy-start.4
  57.2 7.2 %copy-start.3 = (f32[1,64,128]{2,1,0:T(8,128)S(1)}, f32[1,64,128]{2,1,0:T(8,128)}, u32[]{:S(2)}) copy-start(f32[1,64,128]{2,1,0:T(8,128)} %param.11) | copy-start | bytes 98308
  57.2 24.5 %all-to-all-start.2 = ((bf16[16,64,256]{2,1,0:T(8,128)(2,1)}), bf16[16,64,256]{2,1,0:T(8,128)(2,1)S(1)}, u32[]{:S(2)}, u32[]{:S(2)}) async-start(bf16[16,64,256]{2,1,0:T(8,128)(2,1)} %stack.12), calls=%async_computation.2 | async-start | bytes 1048576 | tf_op jit(solution)/shard_map/all_to_all | solution.py:11
  64.3 17.4 %collective-permute-start = (f32[64,128]{1,0:T(8,128)S(1)}, f32[64,128]{1,0:T(8,128)S(1)}, u32[]{:S(2)}, u32[]{:S(2)}) collective-permute-start(f32[64,128]{1,0:T(8,128)S(1)} %bitcast.44), channel_id=1, source_target_pairs={{32,0},{64,32},{96,64},{128,96},{160,128},{192,160},{224,192},{256... | collective-permute-start | bytes 98312 | tf_op jit(solution)/shard_map/ppermute | solution.py:49
  81.7 0.7 copy-start.2
  122.7 24.8 %all-to-all-start.5 = ((bf16[16,64,256]{2,1,0:T(8,128)(2,1)}), bf16[16,64,256]{2,1,0:T(8,128)(2,1)S(1)}, u32[]{:S(2)}, u32[]{:S(2)}) async-start(bf16[16,64,256]{2,1,0:T(8,128)(2,1)} %stack.13), calls=%async_computation.5 | async-start | bytes 1048576 | tf_op jit(solution)/shard_map/all_to_all | solution.py:11
  130.1 17.7 %collective-permute-start.1 = (f32[64,128]{1,0:T(8,128)S(1)}, f32[64,128]{1,0:T(8,128)S(1)}, u32[]{:S(2)}, u32[]{:S(2)}) collective-permute-start(f32[64,128]{1,0:T(8,128)S(1)} %get-tuple-element.8), channel_id=1, source_target_pairs={{32,0},{64,32},{96,64},{128,96},{160,128},{192,160},{224,192},{256... | collective-permute-start | bytes 98312 | tf_op jit(solution)/shard_map/ppermute | solution.py:49
  187.8 24.8 %all-to-all-start.8 = ((bf16[16,64,256]{2,1,0:T(8,128)(2,1)}), bf16[16,64,256]{2,1,0:T(8,128)(2,1)S(1)}, u32[]{:S(2)}, u32[]{:S(2)}) async-start(bf16[16,64,256]{2,1,0:T(8,128)(2,1)} %stack.15), calls=%async_computation.8 | async-start | bytes 1048576 | tf_op jit(solution)/shard_map/all_to_all | solution.py:11
  195.3 17.6 %collective-permute-start.2 = (f32[64,128]{1,0:T(8,128)S(1)}, f32[64,128]{1,0:T(8,128)S(1)}, u32[]{:S(2)}, u32[]{:S(2)}) collective-permute-start(f32[64,128]{1,0:T(8,128)S(1)} %get-tuple-element.3), channel_id=1, source_target_pairs={{32,0},{64,32},{96,64},{128,96},{160,128},{192,160},{224,192},{256... | collective-permute-start | bytes 98312 | tf_op jit(solution)/shard_map/ppermute | solution.py:49
